TPU v7x, 128 devices: a whole 4x4x4 slice. The times are simulated.
128 devices in a mesh: grp: 16 (over x_lo, y, core), freq: 8 (over x_hi, z).
Axes of the slice: x: 4 (x_hi: 2, x_lo: 2; x = x_hi * 2 + x_lo), y: 4, z: 4, core: 2. Of those that a mesh axis runs over, the one named last changes fastest.
Arguments:
- records: bfloat16 [64, 8192, 512], P(None, ('grp', 'freq')), may hold values from -60000 to 60000
- plan: int32 [2], replicated, may hold values from 1 to 15, as said below
Outputs:
- within_spectra: bfloat16 [16, 64, 10, 128, 256], P('grp', 'freq')
- round_spectra: bfloat16 [16, 2, 64, 8, 128, 256], P('grp', None, 'freq')
Inputs may be any that keep to these rules, and one draw needn't show every extreme that they name: `plan`: the masks of different rounds differ.
All inputs are finite; a program needn't handle non-finite values.
Results may differ from a plain program's by a relative error of at most 0.0058.
Values may be sent and summed in bfloat16 or wider, within the bound.
A program may use at most 128 MiB of HBM per device.

v0:
```python
import jax
import jax.numpy as jnp
from jax import lax
from jax.sharding import PartitionSpec as P

GSTA = 128
W = 256
GPD = 4
ROUNDS = 2


EPS = 1e-06


def swapped(x, axis, apart):
    return lax.ppermute(x, axis, [(i, i ^ 1 << apart) for i in range(lax.axis_size(axis))])


def pack_right(block):
    half = block.shape[-1] // 2
    turned = jnp.concatenate([-block[..., half:], block[..., :half]], -1)
    return jnp.concatenate([block, turned], -2)


def cross_spectra(left, right):
    product = jnp.einsum(
        "flsw,frtw->flrst", left, pack_right(right), preferred_element_type=jnp.float32
    )
    scaled = product * W ** (-0.5)
    shape = scaled.shape
    return scaled.reshape(shape[0], shape[1] * shape[2], shape[3], shape[4]).astype(jnp.bfloat16)


def digit_sequence(bit_count):
    return list(range(bit_count))


def fetch_partner(held_block, round_mask, bit_count):
    for bit_number in digit_sequence(bit_count):
        moved_block = swapped(held_block, "grp", bit_number)
        taken = jnp.right_shift(round_mask, bit_number) & 1 == 1
        held_block = jnp.where(taken, moved_block, held_block)
    return held_block


def body(records, plan):
    regrouped = lax.all_to_all(records, "freq", split_axis=0, concat_axis=1, tiled=True)
    values = regrouped.astype(jnp.float32)
    power_sum = jnp.sum(values * values, -1, keepdims=True) / W
    white = (values * lax.rsqrt(power_sum + EPS)).astype(jnp.bfloat16)
    local_freqs = white.shape[0]
    own_groups = white.reshape(local_freqs, GPD, GSTA, 2 * W)
    within = jnp.concatenate(
        [
            cross_spectra(own_groups[:, first : first + 1], own_groups[:, first:])
            for first in range(GPD)
        ],
        1,
    )
    my_index = lax.axis_index("grp")
    group_count = lax.axis_size("grp")
    bit_count = group_count.bit_length() - 1
    rounds_out = []
    for round_step in range(ROUNDS):
        round_mask = plan[round_step]
        partner = fetch_partner(own_groups, round_mask, bit_count)
        partner_index = jnp.bitwise_xor(my_index, round_mask)
        pair_block = lax.cond(
            my_index < partner_index,
            lambda: cross_spectra(own_groups[:, : GPD // 2], partner),
            lambda: cross_spectra(own_groups, partner[:, GPD // 2 :]),
        )
        rounds_out.append(pair_block)
    return (within[None], jnp.stack(rounds_out)[None])


def solution(mesh):
    placed = (P(None, ("grp", "freq"), None), P())
    return jax.shard_map(
        body,
        mesh=mesh,
        in_specs=placed,
        out_specs=(P("grp", "freq", None, None, None), P("grp", None, "freq", None, None, None)),
        check_vma=False,
    )
```

profile of v0, /device:TPU:1, one launch (start us, length us, event | category | flops | bytes accessed | tf_op | source)
XLA Modules:
  0.0 589.5 jit_solution(16716788485438812839)
XLA Ops:
  0.6 57.6 %all_to_all.4 = bf16[64,64,512]{2,1,0:T(8,128)(2,1)S(1)} all-to-all(bf16[64,64,512]{2,1,0:T(8,128)(2,1)} %param.6), channel_id=1, replica_groups=mesh['grp'=16,'freq'=8] {'freq'}, dimensions={0} | all-to-all | bytes 8388608 | tf_op jit(solution)/shard_map/all_to_all | solution.py:47
  58.3 1.2 convert_element_type.140
  59.4 4.5 copy.38
  63.9 0.9 multiply_reduce_fusion
  64.8 0.1 rsqrt.12
  64.9 0.0 copy-start.3
  64.9 5.1 fusion.32
  70.1 2.5 collective-permute-start
  72.6 0.0 copy-done.3
  72.6 0.6 fusion.60
  74.4 5.3 collective-permute-done
  79.7 8.0 %broadcast_select_fusion.4 = (bf16[8,4,128,512]{3,2,0,1:T(8,128)(2,1)}, bf16[8,4,128,512]{3,2,0,1:T(8,128)(2,1)}) fusion(bf16[8,4,128,512]{3,2,0,1:T(8,128)(2,1)} %collective-permute-done, pred[]{:T(512)S(6)} %eq.27, pred[]{:T(512)S(6)} %eq.31, f32[8,4,128]{2,0,1:T(8,128)S(1)} %copy.40, f32[8,4,128,512]{3,2,1,0:T(8,128)} %bitcast.135), kind=kLoop, calls=%fused_computation.59 | loop fusion | flops 8388608 | bytes 20987906 | tf_op jit(solution)/shard_map/jit(_where)/select_n | solution.py:42
  87.6 1.3 collective-permute-start.1
  88.9 0.2 collective-permute-start.4
  90.4 89.4 %collective-permute-done.1 = bf16[8,4,128,512]{3,2,0,1:T(8,128)(2,1)} collective-permute-done((bf16[8,4,128,512]{3,2,0,1:T(8,128)(2,1)}, bf16[8,4,128,512]{3,2,0,1:T(8,128)(2,1)}, u32[]{:S(2)}, u32[]{:S(2)}) %collective-permute-start.1) | collective-permute-done | bytes 4194336 | tf_op jit(solution)/shard_map/ppermute | solution.py:16
  179.7 4.6 broadcast_select_fusion.5
  184.4 2.9 collective-permute-start.2
  187.3 82.3 %collective-permute-done.4 = bf16[8,4,128,512]{3,2,0,1:T(8,128)(2,1)} collective-permute-done((bf16[8,4,128,512]{3,2,0,1:T(8,128)(2,1)}, bf16[8,4,128,512]{3,2,0,1:T(8,128)(2,1)}, u32[]{:S(2)}, u32[]{:S(2)}) %collective-permute-start.4) | collective-permute-done | bytes 4194336 | tf_op jit(solution)/shard_map/ppermute | solution.py:16
  269.6 4.6 broadcast_select_fusion.1
  274.3 2.9 collective-permute-start.5
  281.0 1.3 slice.134
  282.3 1.3 slice_negate_fusion.7
  283.5 0.7 fusion.57
  284.2 77.7 %collective-permute-done.2 = bf16[8,4,128,512]{3,2,0,1:T(8,128)(2,1)} collective-permute-done((bf16[8,4,128,512]{3,2,0,1:T(8,128)(2,1)}, bf16[8,4,128,512]{3,2,0,1:T(8,128)(2,1)}, u32[]{:S(2)}, u32[]{:S(2)}) %collective-permute-start.2) | collective-permute-done | bytes 4194336 | tf_op jit(solution)/shard_map/ppermute | solution.py:16
  362.0 4.6 broadcast_select_fusion.6
  366.5 0.9 collective-permute-start.3
  367.4 84.4 %collective-permute-done.5 = bf16[8,4,128,512]{3,2,0,1:T(8,128)(2,1)} collective-permute-done((bf16[8,4,128,512]{3,2,0,1:T(8,128)(2,1)}, bf16[8,4,128,512]{3,2,0,1:T(8,128)(2,1)}, u32[]{:S(2)}, u32[]{:S(2)}) %collective-permute-start.5) | collective-permute-done | bytes 4194336 | tf_op jit(solution)/shard_map/ppermute | solution.py:16
  451.8 4.6 broadcast_select_fusion.2
  456.4 0.9 collective-permute-start.6
  457.3 1.7 slice_negate_fusion.6
  459.0 2.1 slice.126
  461.1 1.7 slice.130
  462.8 2.1 slice_negate_fusion.5
  464.9 2.5 slice_negate_fusion.4
  467.4 2.7 fusion.52
  470.1 3.0 fusion.49
  473.2 4.2 fusion.37
  477.4 3.0 maximum_bitcast_fusion.17
  480.4 7.8 %copy.53 = bf16[1,8,10,128,256]{4,3,2,1,0:T(8,128)(2,1)} copy(bf16[1,8,10,128,256]{3,4,2,1,0:T(8,128)(2,1)} %maximum_bitcast_fusion.17) | data formatting | bytes 10485760
  488.2 0.0 collective-permute-done.3
  488.2 2.6 broadcast_select_fusion.7
  490.9 56.7 %collective-permute-done.6 = bf16[8,4,128,512]{3,2,0,1:T(8,128)(2,1)} collective-permute-done((bf16[8,4,128,512]{3,2,0,1:T(8,128)(2,1)}, bf16[8,4,128,512]{3,2,0,1:T(8,128)(2,1)}, u32[]{:S(2)}, u32[]{:S(2)}) %collective-permute-start.6) | collective-permute-done | bytes 4194336 | tf_op jit(solution)/shard_map/ppermute | solution.py:16
  547.6 4.6 broadcast_select_fusion.3
  552.3 14.6 %conditional.12 = (bf16[1,8,8,128,256]{4,3,2,1,0:T(8,128)(2,1)}) conditional(s32[]{:T(128)} %convert_element_type.134, (bf16[8,4,128,512]{3,2,0,1:T(8,128)(2,1)S(1)}, bf16[8,4,128,512]{3,2,0,1:T(8,128)(2,1)}) %tuple.40, (bf16[8,4,128,512]{3,2,0,1:T(8,128)(2,1)S(1)}, bf16[8,4,128,512]{3,2,0,1:T(8,128)(2,1)}) %tuple.40), branch_computations={%region_1.2_spmd, %region_2.3_spmd} | conditional | flops 2179989504 | bytes 48234532
  552.3 0.0 copy-start.2
  552.3 0.7 slice_negate_fusion.1
  553.0 1.3 copy-done.2
  554.2 6.1 %multiply_bitcast_fusion.1 = bf16[8,2,4,128,256]{3,4,1,2,0:T(8,128)(2,1)} fusion(bf16[8,4,128,256]{3,2,1,0:T(8,128)(2,1)S(1)} %get-tuple-element.77, bf16[8,4,128,256]{3,2,1,0:T(8,128)(2,1)S(1)} %get-tuple-element.76, bf16[8,4,128,512]{3,2,0,1:T(8,128)(2,1)} %get-tuple-element.67, bf16[8,4,128,512]{3,2,0,1:T(8,128)(2,1)} %copy-done.2), kind=kOutput, calls=%fused_computation.16 | convolution fusion | flops 2176843776 | bytes 14680064 | tf_op jit(solution)/shard_map/cond/branch_1_fun/flsw,frtw->flrst/dot_general | solution.py:26
  560.4 6.5 %copy.35 = bf16[8,2,4,128,256]{4,3,2,1,0:T(8,128)(2,1)} copy(bf16[8,2,4,128,256]{3,4,1,2,0:T(8,128)(2,1)} %multiply_bitcast_fusion.1) | data formatting | bytes 8388608 | tf_op jit(solution)/shard_map/cond/branch_1_fun/mul | solution.py:29
  566.8 15.1 %conditional.13 = (bf16[1,8,8,128,256]{4,3,2,1,0:T(8,128)(2,1)}) conditional(s32[]{:T(128)} %convert_element_type.136, (bf16[8,4,128,512]{3,2,0,1:T(8,128)(2,1)}, bf16[8,4,128,512]{3,2,0,1:T(8,128)(2,1)}) %tuple.41, (bf16[8,4,128,512]{3,2,0,1:T(8,128)(2,1)}, bf16[8,4,128,512]{3,2,0,1:T(8,128)(2,1)}) %tuple.41), branch_computations={%region_3.4_spmd, %region_4.5_spmd} | conditional | flops 2179989504 | bytes 54525988
  566.8 0.0 copy-start.1
  566.8 3.0 slice_negate_fusion.3
  569.8 0.4 copy-done.1
  570.3 5.2 multiply_bitcast_fusion.3
  575.5 6.4 %copy.37 = bf16[8,2,4,128,256]{4,3,2,1,0:T(8,128)(2,1)} copy(bf16[8,2,4,128,256]{3,4,1,2,0:T(8,128)(2,1)} %multiply_bitcast_fusion.3) | data formatting | bytes 8388608 | tf_op jit(solution)/shard_map/cond/branch_1_fun/mul | solution.py:29
  581.9 7.6 %maximum_bitcast_fusion.16 = bf16[1,2,8,8,128,256]{5,4,3,2,1,0:T(8,128)(2,1)} fusion(bf16[1,8,8,128,256]{4,3,2,1,0:T(8,128)(2,1)} %get-tuple-element.95, bf16[1,8,8,128,256]{4,3,2,1,0:T(8,128)(2,1)} %get-tuple-element.94), kind=kLoop, calls=%fused_computation.41 | loop fusion | flops 4194304 | bytes 16777216 | tf_op jit(solution)/shard_map/broadcast_in_dim | solution.py:74
  (3 shorter events, 0.0 us)
Async XLA Ops:
  64.9 7.7 %copy-start.3 = (s32[2]{0:T(128)S(1)}, s32[2]{0:T(128)}, u32[]{:S(2)}) copy-start(s32[2]{0:T(128)} %param.7) | copy-start | bytes 28
  70.1 9.6 %collective-permute-start = (bf16[8,4,128,512]{3,2,0,1:T(8,128)(2,1)}, bf16[8,4,128,512]{3,2,0,1:T(8,128)(2,1)}, u32[]{:S(2)}, u32[]{:S(2)}) collective-permute-start(bf16[8,4,128,512]{3,2,0,1:T(8,128)(2,1)} %fusion.32), channel_id=1, source_target_pairs={{0,8},{8,0},{16,24},{24,16},{32,40},{40,32},{48,56},{56,48},{64,72... | collective-permute-start | bytes 12582920 | tf_op jit(solution)/shard_map/ppermute | solution.py:16
  87.6 92.1 %collective-permute-start.1 = (bf16[8,4,128,512]{3,2,0,1:T(8,128)(2,1)}, bf16[8,4,128,512]{3,2,0,1:T(8,128)(2,1)}, u32[]{:S(2)}, u32[]{:S(2)}) collective-permute-start(bf16[8,4,128,512]{3,2,0,1:T(8,128)(2,1)} %get-tuple-element.82), channel_id=1, source_target_pairs={{0,16},{8,24},{16,0},{24,8},{32,48},{40,56},{48,32},{56,40},{64,80... | collective-permute-start | bytes 12582920 | tf_op jit(solution)/shard_map/ppermute | solution.py:16
  88.9 180.7 %collective-permute-start.4 = (bf16[8,4,128,512]{3,2,0,1:T(8,128)(2,1)}, bf16[8,4,128,512]{3,2,0,1:T(8,128)(2,1)}, u32[]{:S(2)}, u32[]{:S(2)}) collective-permute-start(bf16[8,4,128,512]{3,2,0,1:T(8,128)(2,1)} %get-tuple-element.83), channel_id=1, source_target_pairs={{0,16},{8,24},{16,0},{24,8},{32,48},{40,56},{48,32},{56,40},{64,80... | collective-permute-start | bytes 12582920 | tf_op jit(solution)/shard_map/ppermute | solution.py:16
  184.4 177.6 %collective-permute-start.2 = (bf16[8,4,128,512]{3,2,0,1:T(8,128)(2,1)}, bf16[8,4,128,512]{3,2,0,1:T(8,128)(2,1)}, u32[]{:S(2)}, u32[]{:S(2)}) collective-permute-start(bf16[8,4,128,512]{3,2,0,1:T(8,128)(2,1)} %broadcast_select_fusion.5), channel_id=1, source_target_pairs={{0,32},{8,40},{16,48},{24,56},{32,0},{40,8},{48,16},{56,24},{64,96... | collective-permute-start | bytes 12582920 | tf_op jit(solution)/shard_map/ppermute | solution.py:16
  274.3 177.6 %collective-permute-start.5 = (bf16[8,4,128,512]{3,2,0,1:T(8,128)(2,1)}, bf16[8,4,128,512]{3,2,0,1:T(8,128)(2,1)}, u32[]{:S(2)}, u32[]{:S(2)}) collective-permute-start(bf16[8,4,128,512]{3,2,0,1:T(8,128)(2,1)} %broadcast_select_fusion.1), channel_id=1, source_target_pairs={{0,32},{8,40},{16,48},{24,56},{32,0},{40,8},{48,16},{56,24},{64,96... | collective-permute-start | bytes 12582920 | tf_op jit(solution)/shard_map/ppermute | solution.py:16
  366.5 121.7 %collective-permute-start.3 = (bf16[8,4,128,512]{3,2,0,1:T(8,128)(2,1)}, bf16[8,4,128,512]{3,2,0,1:T(8,128)(2,1)}, u32[]{:S(2)}, u32[]{:S(2)}) collective-permute-start(bf16[8,4,128,512]{3,2,0,1:T(8,128)(2,1)} %broadcast_select_fusion.6), channel_id=1, source_target_pairs={{0,64},{8,72},{16,80},{24,88},{32,96},{40,104},{48,112},{56,120},{... | collective-permute-start | bytes 12582920 | tf_op jit(solution)/shard_map/ppermute | solution.py:16
  456.4 91.2 %collective-permute-start.6 = (bf16[8,4,128,512]{3,2,0,1:T(8,128)(2,1)}, bf16[8,4,128,512]{3,2,0,1:T(8,128)(2,1)}, u32[]{:S(2)}, u32[]{:S(2)}) collective-permute-start(bf16[8,4,128,512]{3,2,0,1:T(8,128)(2,1)} %broadcast_select_fusion.2), channel_id=1, source_target_pairs={{0,64},{8,72},{16,80},{24,88},{32,96},{40,104},{48,112},{56,120},{... | collective-permute-start | bytes 12582920 | tf_op jit(solution)/shard_map/ppermute | solution.py:16
  552.3 2.0 copy-start.2
  566.8 3.4 copy-start.1
where the time goes:
time: 592 us; the launch traced here: 590 us
  waiting for transfers between devices  396 us (67%)
  other arithmetic  62.7 us (11%)
  blocking collectives  57.6 us (10%)
  local copies, waits for them, and re-layouts  32.7 us (6%)
  matrix products  22 us (4%)
  starting transfers between devices  11.6 us (2%)
  between operations  7.05 us (1%)
    ppermute x7, waiting for transfers between devices, swapped(): lax.ppermute(x, axis, [(i, i ^ 1 << apart) for i in range(lax.axis_size(a...  396 us
    all_to_all x1, blocking collectives, body(): lax.all_to_all(records, 'freq', split_axis=0, concat_axis=1, tiled=True)  57.6 us
    select_n x7, other arithmetic, fetch_partner(): held_block = jnp.where(taken, moved_block, held_block)  33.6 us
    dot_general x6, matrix products, cross_spectra(): jnp.einsum('flsw,frtw->flrst', left, pack_right(right), preferred_element...  22 us
    mul x2, local copies, waits for them, and re-layouts, cross_spectra(): scaled = product * W ** (-0.5)  12.9 us
  transfers between devices with their start and end apart: 7, of which 6 were waited for; matrix products, arithmetic and copies ran while one was open for 9% of the time, Pallas kernels for 0%

commit v1 on v0

v1 whole, which is shorter than its diff:
```python
import functools

import jax
import jax.numpy as jnp
from jax import lax
from jax.experimental import pallas as pl
from jax.experimental.pallas import tpu as pltpu
from jax.sharding import PartitionSpec as P

GSTA = 128
W = 256
GPD = 4
ROUNDS = 2
N_GRP = 16
EPS = 1e-06


def turned(block):
    return jnp.concatenate([-block[:, W:], block[:, :W]], -1)


def times(left, right):
    return lax.dot_general(left, right, (((1,), (1,)), ((), ())), preferred_element_type=jnp.float32)


def spectra_kernel(lower_ref, own_ref, partner_ref, within_ref, round_ref):
    own = own_ref.at[0]

    def cross(rows, right_ref, start):
        right = right_ref[pl.ds(start, GSTA), :]
        packed = jnp.concatenate([right, turned(right)], 0)
        return (times(own[pl.ds(0, rows), :], packed) * W ** (-0.5)).astype(jnp.bfloat16)

    pairs = [(i, j) for i in range(GPD) for j in range(i, GPD)]
    for j in range(GPD):
        product = cross((j + 1) * GSTA, own, j * GSTA)
        for i in range(j + 1):
            within_ref[0, 0, pairs.index((i, j))] = product[i * GSTA : (i + 1) * GSTA]
    for r in range(ROUNDS):
        partner = partner_ref.at[r, 0]

        @pl.when(lower_ref[r] == 1)
        def _():
            for j in range(GPD):
                product = cross(2 * GSTA, partner, j * GSTA)
                for i in range(2):
                    round_ref[0, r, 0, i * GPD + j] = product[i * GSTA : (i + 1) * GSTA]

        @pl.when(lower_ref[r] == 0)
        def _():
            for j in range(2):
                product = cross(GPD * GSTA, partner, (2 + j) * GSTA)
                for i in range(GPD):
                    round_ref[0, r, 0, i * 2 + j] = product[i * GSTA : (i + 1) * GSTA]


def spectra(lower, own, partner):
    freqs, stations, width = own.shape
    return pl.pallas_call(
        spectra_kernel,
        grid_spec=pltpu.PrefetchScalarGridSpec(
            num_scalar_prefetch=1,
            grid=(freqs,),
            in_specs=[
                pl.BlockSpec((1, stations, width), lambda f, _: (f, 0, 0)),
                pl.BlockSpec((ROUNDS, 1, stations, width), lambda f, _: (0, f, 0, 0)),
            ],
            out_specs=[
                pl.BlockSpec((1, 1, 10, GSTA, 2 * GSTA), lambda f, _: (0, f, 0, 0, 0)),
                pl.BlockSpec((1, ROUNDS, 1, 8, GSTA, 2 * GSTA), lambda f, _: (0, 0, f, 0, 0, 0)),
            ],
        ),
        out_shape=[
            jax.ShapeDtypeStruct((1, freqs, 10, GSTA, 2 * GSTA), jnp.bfloat16),
            jax.ShapeDtypeStruct((1, ROUNDS, freqs, 8, GSTA, 2 * GSTA), jnp.bfloat16),
        ],
        compiler_params=pltpu.CompilerParams(vmem_limit_bytes=48 * 1024 * 1024),
        cost_estimate=pl.CostEstimate(flops=7 * 10**9, bytes_accessed=27 * 10**6, transcendentals=0),
        name="spectra",
    )(lower, own, partner)


def fetch(own, mask):
    def by(m):
        return lambda: lax.ppermute(own, "grp", [(i, i ^ m) for i in range(N_GRP)])

    return lax.switch(mask - 1, [by(m) for m in range(1, N_GRP)])


def body(records, plan):
    regrouped = lax.all_to_all(records, "freq", split_axis=0, concat_axis=1, tiled=True)
    values = regrouped.astype(jnp.float32)
    power_sum = jnp.sum(values * values, -1, keepdims=True) / W
    white = (values * lax.rsqrt(power_sum + EPS)).astype(jnp.bfloat16)
    me = lax.axis_index("grp")
    partner = jnp.stack([fetch(white, plan[r]) for r in range(ROUNDS)])
    lower = (me < jnp.bitwise_xor(me, plan)).astype(jnp.int32)
    within, rounds = spectra(lower, white, partner)
    return within, rounds


def solution(mesh):
    placed = (P(None, ("grp", "freq"), None), P())
    return jax.shard_map(
        body,
        mesh=mesh,
        in_specs=placed,
        out_specs=(P("grp", "freq", None, None, None), P("grp", None, "freq", None, None, None)),
        check_vma=False,
    )
```

time: 592 us -> 283 us (0.48)
  waiting for transfers between devices: 396 us -> 228 us
  blocking collectives: 57.6 us -> 0 us
  other arithmetic: 62.7 us -> 12 us
  local copies, waits for them, and re-layouts: 32.7 us -> 8.08 us
  matrix products: 22 us -> 0 us
  Pallas kernels: 0 us -> 16.4 us
    ppermute x7 -> x2, waiting for transfers between devices: 396 us -> 181 us  [by(): return lambda: lax.ppermute(own, 'grp', [(i, i ^ m) for i in range(N_GRP)])]
    all_to_all x1 -> x0, blocking collectives: 57.6 us -> none  [body(): lax.all_to_all(records, 'freq', split_axis=0, concat_axis=1, tiled=True)]
    all_to_all x0 -> x1, waiting for transfers between devices: none -> 46.8 us  [body(): lax.all_to_all(records, 'freq', split_axis=0, concat_axis=1, tiled=True)]
    select_n x7 -> x0, other arithmetic: 33.6 us -> none  [fetch_partner(): held_block = jnp.where(taken, moved_block, held_block)]
    dot_general x6 -> x0, matrix products: 22 us -> none  [cross_spectra(): jnp.einsum('flsw,frtw->flrst', left, pack_right(right), preferred_element...]
    pallas_call x0 -> x1, Pallas kernels: none -> 16.4 us  [spectra(): pl.pallas_call(spectra_kernel, grid_spec=pltpu.PrefetchScalarGridSpec(num...]
    mul x2 -> x0, local copies, waits for them, and re-layouts: 12.9 us -> none  [cross_spectra(): scaled = product * W ** (-0.5)]
    neg x6 -> x0, other arithmetic: 11.2 us -> none  [pack_right(): turned = jnp.concatenate([-block[..., half:], block[..., :half]], -1)]
  transfers between devices with their start and end apart: 7 -> 3, of which waited for: 6 -> 3; matrix products, arithmetic and copies ran while one was open for 9% -> 0% of each run, Pallas kernels for 0% -> 0%
where the time goes in v1:
time: 283 us
  waiting for transfers between devices  228 us (81%)
  Pallas kernels  16.4 us (6%)
  starting transfers between devices  15.9 us (6%)
  other arithmetic  12 us (4%)
  local copies, waits for them, and re-layouts  8.08 us (3%)
    ppermute x2, waiting for transfers between devices, by(): return lambda: lax.ppermute(own, 'grp', [(i, i ^ m) for i in range(N_GRP)])  181 us
    all_to_all x1, waiting for transfers between devices, body(): lax.all_to_all(records, 'freq', split_axis=0, concat_axis=1, tiled=True)  46.8 us
    pallas_call x1, Pallas kernels, spectra(): pl.pallas_call(spectra_kernel, grid_spec=pltpu.PrefetchScalarGridSpec(num...  16.4 us
    all_to_all x1, starting transfers between devices, body(): lax.all_to_all(records, 'freq', split_axis=0, concat_axis=1, tiled=True)  8.34 us
    another operation x1, other arithmetic, body(): partner = jnp.stack([fetch(white, plan[r]) for r in range(ROUNDS)])  7.67 us
    ppermute x2, starting transfers between devices, by(): return lambda: lax.ppermute(own, 'grp', [(i, i ^ m) for i in range(N_GRP)])  7.56 us
  transfers between devices with their start and end apart: 3, of which 3 were waited for; matrix products, arithmetic and copies ran while one was open for 0% of the time, Pallas kernels for 0%

profile of v1, /device:TPU:1, one launch (start us, length us, event | category | flops | bytes accessed | tf_op | source)
XLA Modules:
  0.0 282.7 jit_solution(14953494805733253691)
XLA Ops:
  0.6 0.0 copy-start.17
  0.6 8.3 %all-to-all-start = ((bf16[64,64,512]{2,1,0:T(8,128)(2,1)}), bf16[64,64,512]{2,1,0:T(8,128)(2,1)}, u32[]{:S(2)}, u32[]{:S(2)}) async-start(bf16[64,64,512]{2,1,0:T(8,128)(2,1)} %param.32), calls=%async_computation | async-start | bytes 8388608 | tf_op jit(solution)/shard_map/all_to_all | solution.py:91
  9.0 0.0 copy-done.17
  9.0 0.6 fusion.1
  10.9 46.8 %all-to-all-done = bf16[64,64,512]{2,1,0:T(8,128)(2,1)} async-done(((bf16[64,64,512]{2,1,0:T(8,128)(2,1)}), bf16[64,64,512]{2,1,0:T(8,128)(2,1)}, u32[]{:S(2)}, u32[]{:S(2)}) %all-to-all-start) | async-done | bytes 4194336 | tf_op jit(solution)/shard_map/all_to_all | solution.py:91
  57.7 3.1 %multiply_reduce_fusion = f32[64,64]{1,0:T(8,128)S(1)} fusion(bf16[64,64,512]{2,1,0:T(8,128)(2,1)} %all-to-all-done), kind=kLoop, calls=%fused_computation.3 | loop fusion | flops 6287360 | bytes 4210688 | tf_op jit(solution)/shard_map/reduce_sum | solution.py:93
  60.8 0.1 rsqrt.12
  60.9 3.4 %copy.6 = f32[8,8,64,512]{3,2,0,1:T(8,128)S(1)} copy(bf16[8,8,64,512]{3,2,1,0:T(8,128)(2,1)} %bitcast.43) | data formatting | bytes 12582912 | tf_op jit(solution)/shard_map/convert_element_type | solution.py:92
  64.3 1.3 fusion.own_ref
  65.6 0.0 copy-start
  65.6 2.0 copy-done
  67.6 95.0 %conditional.3 = (bf16[1,8,512,512]{3,2,1,0:T(8,128)(2,1)}) conditional(s32[]{:T(128)} %bitcast.36, bf16[8,512,512]{2,1,0:T(8,128)(2,1)S(1)} %fusion.own_ref, bf16[8,512,512]{2,1,0:T(8,128)(2,1)S(1)} %fusion.own_ref, bf16[8,512,512]{2,1,0:T(8,128)(2,1)S(1)} %fusion.own_ref, ...), branch_computations={%region_16.0_spmd, %region_17.0_spmd, %region_18.0_spmd, %region_1... | conditional | bytes 33554508 | solution.py:87
  67.6 2.8 collective-permute-start.28
  70.3 90.2 %collective-permute-done.28 = bf16[8,512,512]{2,1,0:T(8,128)(2,1)S(1)} collective-permute-done((bf16[8,512,512]{2,1,0:T(8,128)(2,1)S(1)}, bf16[8,512,512]{2,1,0:T(8,128)(2,1)S(1)}, u32[]{:S(2)}, u32[]{:S(2)}) %collective-permute-start.28) | collective-permute-done | bytes 4194336 | tf_op jit(solution)/shard_map/cond/branch_13_fun/ppermute | solution.py:85
  160.5 0.0 copy-start.15
  160.5 2.0 copy-done.15
  162.5 96.1 %conditional.2 = (bf16[1,8,512,512]{3,2,1,0:T(8,128)(2,1)}) conditional(s32[]{:T(128)} %bitcast.35, bf16[8,512,512]{2,1,0:T(8,128)(2,1)} %copy-done, bf16[8,512,512]{2,1,0:T(8,128)(2,1)} %copy-done, bf16[8,512,512]{2,1,0:T(8,128)(2,1)} %copy-done, bf16[8,512,512]{2,1,0:T(8,128)(2,1)} %copy-done, ...), branch_computations={%region_1.0_spmd, %region_2.0_spmd, %region_3.0_spmd, %region_4.0_... | conditional | bytes 16777264 | solution.py:87
  162.5 4.8 %collective-permute-start.14 = (bf16[8,512,512]{2,1,0:T(8,128)(2,1)}, bf16[8,512,512]{2,1,0:T(8,128)(2,1)}, u32[]{:S(2)}, u32[]{:S(2)}) collective-permute-start(bf16[8,512,512]{2,1,0:T(8,128)(2,1)} %param.14), channel_id=1, source_target_pairs={{0,120},{8,112},{16,104},{24,96},{32,88},{40,80},{48,72},{56,64},{... | collective-permute-start | bytes 12582920 | tf_op jit(solution)/shard_map/cond/branch_14_fun/ppermute | solution.py:85
  167.3 91.3 %collective-permute-done.14 = bf16[8,512,512]{2,1,0:T(8,128)(2,1)} collective-permute-done((bf16[8,512,512]{2,1,0:T(8,128)(2,1)}, bf16[8,512,512]{2,1,0:T(8,128)(2,1)}, u32[]{:S(2)}, u32[]{:S(2)}) %collective-permute-start.14) | collective-permute-done | bytes 4194336 | tf_op jit(solution)/shard_map/cond/branch_14_fun/ppermute | solution.py:85
  258.6 0.0 copy-start.1
  258.6 7.7 %pad_maximum_fusion.partner_ref = bf16[2,8,512,512]{3,2,1,0:T(8,128)(2,1)} fusion(bf16[1,8,512,512]{3,2,1,0:T(8,128)(2,1)} %get-tuple-element.69, bf16[1,8,512,512]{3,2,1,0:T(8,128)(2,1)} %get-tuple-element.68), kind=kLoop, calls=%fused_computation | loop fusion | flops 4194304 | bytes 16777216 | tf_op jit(solution)/shard_map/stack | solution.py:96
  266.3 0.0 copy-done.1
  266.3 16.4 %spectra.1 = (bf16[1,8,10,128,256]{4,3,2,1,0:T(8,128)(2,1)}, bf16[1,2,8,8,128,256]{5,4,3,2,1,0:T(8,128)(2,1)}) custom-call(s32[2]{0:T(128)S(1)} %compare_convert_fusion.lower_ref, bf16[8,512,512]{2,1,0:T(8,128)(2,1)S(1)} %copy-done.1, bf16[2,8,512,512]{3,2,1,0:T(8,128)(2,1)} %pad_maximum_fusion.partner_ref), custom_call_target="tpu_custom_call" | custom-call | flops 7000000000 | bytes 27000000 | tf_op jit(solution)/shard_map/spectra/pallas_call | solution.py:59
  (3 shorter events, 0.0 us)
Async XLA Ops:
  0.6 8.3 %copy-start.17 = (s32[2]{0:T(128)S(1)}, s32[2]{0:T(128)}, u32[]{:S(2)}) copy-start(s32[2]{0:T(128)} %param.33) | copy-start | bytes 28
  0.6 57.1 %all-to-all-start = ((bf16[64,64,512]{2,1,0:T(8,128)(2,1)}), bf16[64,64,512]{2,1,0:T(8,128)(2,1)}, u32[]{:S(2)}, u32[]{:S(2)}) async-start(bf16[64,64,512]{2,1,0:T(8,128)(2,1)} %param.32), calls=%async_computation | async-start | bytes 8388608 | tf_op jit(solution)/shard_map/all_to_all | solution.py:91
  65.6 2.0 copy-start
  67.6 93.0 %collective-permute-start.28 = (bf16[8,512,512]{2,1,0:T(8,128)(2,1)S(1)}, bf16[8,512,512]{2,1,0:T(8,128)(2,1)S(1)}, u32[]{:S(2)}, u32[]{:S(2)}) collective-permute-start(bf16[8,512,512]{2,1,0:T(8,128)(2,1)S(1)} %param.28), channel_id=1, source_target_pairs={{0,112},{8,120},{16,96},{24,104},{32,80},{40,88},{48,64},{56,72},{... | collective-permute-start | bytes 12582920 | tf_op jit(solution)/shard_map/cond/branch_13_fun/ppermute | solution.py:85
  160.5 2.0 copy-start.15
  162.5 96.1 %collective-permute-start.14 = (bf16[8,512,512]{2,1,0:T(8,128)(2,1)}, bf16[8,512,512]{2,1,0:T(8,128)(2,1)}, u32[]{:S(2)}, u32[]{:S(2)}) collective-permute-start(bf16[8,512,512]{2,1,0:T(8,128)(2,1)} %param.14), channel_id=1, source_target_pairs={{0,120},{8,112},{16,104},{24,96},{32,88},{40,80},{48,72},{56,64},{... | collective-permute-start | bytes 12582920 | tf_op jit(solution)/shard_map/cond/branch_14_fun/ppermute | solution.py:85
  258.6 7.7 %copy-start.1 = (bf16[8,512,512]{2,1,0:T(8,128)(2,1)S(1)}, bf16[8,512,512]{2,1,0:T(8,128)(2,1)}, u32[]{:S(2)}) copy-start(bf16[8,512,512]{2,1,0:T(8,128)(2,1)} %copy-done) | copy-start | bytes 12582916

commit v2 on v1

--- a/solution.py
+++ b/solution.py
@@ -79,23 +79,203 @@
         name="spectra",
     )(lower, own, partner)
 
-
-def fetch(own, mask):
-    def by(m):
-        return lambda: lax.ppermute(own, "grp", [(i, i ^ m) for i in range(N_GRP)])
-
-    return lax.switch(mask - 1, [by(m) for m in range(1, N_GRP)])
+X_LO = 8
+X_HI = 4
+
+
+def flip(index, size):
+    return index + size - 2 * size * (index // size % 2)
+
+
+def meet(index, bits, size):
+    for bit in (1, 2):
+        if bits & bit:
+            index = flip(index, size * bit)
+    return index
+
+
+def exchange_kernel(
+    hops, plan_ref, rec_ref, own_ref, got_ref, ready, across, blocks, picked,
+    z_out, z_in, x_out, x_in, core_out, core_in, y_out, y_in, own_sem,
+):
+    chunks, _, _, stations, _ = blocks.shape
+    part = rec_ref.shape[1]
+    half = stations // 2
+    g = lax.axis_index("grp")
+    q = lax.axis_index("freq")
+    z = q % 4
+    hi = q // X_HI
+    inner = (flip(g, X_LO), q)
+    outer = (flip(g, X_LO), flip(q, X_HI))
+    mate = (flip(g, 1), q)
+    aside = [(g, meet(q, j, 1)) for j in range(1, 4)]
+    along = [(meet(g, hop, 2), q) for hop in hops]
+    friends = [inner, outer, mate] + aside
+    friends += [along[r] for r in range(ROUNDS) if hops[r] and hops[r] not in hops[:r]]
+
+    barrier = pltpu.get_barrier_semaphore()
+    for friend in friends:
+        pl.semaphore_signal(barrier, inc=1, device_id=friend, device_id_type=pl.DeviceIdType.MESH)
+    pl.semaphore_wait(barrier, len(friends))
+
+    near = pl.ds(pl.multiple_of(hi * half, half), half)
+    far = pl.ds(pl.multiple_of((1 - hi) * half, half), half)
+    near_part = pl.ds(pl.multiple_of(hi * half + z * part, part), part)
+    far_part = pl.ds(pl.multiple_of(z * part, part), part)
+
+    def remote(source, target, sent, landed, device):
+        return pltpu.make_async_remote_copy(
+            src_ref=source, dst_ref=target, send_sem=sent, recv_sem=landed,
+            device_id=device, device_id_type=pl.DeviceIdType.MESH,
+        )
+
+    def z_copies(c):
+        copies = []
+        for j in range(3):
+            copies.append(remote(
+                ready.at[c, j, 0], blocks.at[c, 0, 0, near_part],
+                z_out.at[c, j, 0], z_in.at[c, j, 0], aside[j],
+            ))
+            copies.append(remote(
+                ready.at[c, j, 1], across.at[c, far_part],
+                z_out.at[c, j, 1], z_in.at[c, j, 1], aside[j],
+            ))
+        return copies
+
+    def x_inner(c):
+        return remote(
+            blocks.at[c, 0, 0, near], blocks.at[c, 0, 1, near], x_out.at[c, 0], x_in.at[c, 0], inner
+        )
+
+    def x_outer(c):
+        return remote(across.at[c], blocks.at[c, 0, 1, near], x_out.at[c, 1], x_in.at[c, 1], outer)
+
+    def x_relay(c):
+        return remote(
+            blocks.at[c, 0, 1, far], blocks.at[c, 0, 0, far], x_out.at[c, 2], x_in.at[c, 2], inner
+        )
+
+    def core_copy(c):
+        return remote(blocks.at[c, 0], blocks.at[c, 1], core_out.at[c], core_in.at[c], mate)
+
+    def own_copy(c):
+        return pltpu.make_async_copy(blocks.at[c, 0, 0], own_ref.at[c], own_sem.at[c])
+
+    def y_copy(c, r):
+        if hops[r]:
+            return remote(
+                picked.at[r, c], got_ref.at[r, c], y_out.at[r, c], y_in.at[r, c], along[r]
+            )
+        return pltpu.make_async_copy(picked.at[r, c], got_ref.at[r, c], y_out.at[r, c])
+
+    def whiten(c):
+        for j in range(4):
+            for k in range(2):
+                band = (hi if k == 0 else 1 - hi) * X_HI + meet(z, j, 1)
+                values = rec_ref[band * chunks + c].astype(jnp.float32)
+                power = jnp.sum(values * values, -1, keepdims=True) / W
+                white = (values * lax.rsqrt(power + EPS)).astype(jnp.bfloat16)
+                if j:
+                    ready[c, j - 1, k] = white
+                elif k:
+                    across[c, far_part] = white
+                else:
+                    blocks[c, 0, 0, near_part] = white
+        for copy in z_copies(c):
+            copy.start()
+
+    def spread(c):
+        for copy in z_copies(c):
+            copy.wait_recv()
+        x_inner(c).start()
+        x_outer(c).start()
+
+    def relay(c):
+        x_outer_landed(c).wait_recv()
+        x_relay(c).start()
+
+    def x_outer_landed(c):
+        return remote(across.at[c], blocks.at[c, 0, 1, far], x_out.at[c, 1], x_in.at[c, 1], outer)
+
+    def share(c):
+        x_inner_landed = remote(
+            blocks.at[c, 0, 0, near], blocks.at[c, 0, 1, near], x_out.at[c, 0], x_in.at[c, 0], inner
+        )
+        x_inner_landed.wait_recv()
+        x_relay(c).wait_recv()
+        core_copy(c).start()
+        own_copy(c).start()
+
+    def send(c):
+        core_copy(c).wait_recv()
+        for r in range(ROUNDS):
+            other_lo = plan_ref[r] >= X_LO
+            other_core = plan_ref[r] % 2 == 1
+            here = jnp.where(other_lo, blocks[c, 0, 1], blocks[c, 0, 0])
+            there = jnp.where(other_lo, blocks[c, 1, 1], blocks[c, 1, 0])
+            picked[r, c] = jnp.where(other_core, there, here)
+        for r in range(ROUNDS):
+            y_copy(c, r).start()
+
+    def step(t, carry):
+        for stage, late in ((spread, 1), (whiten, 0), (relay, 2), (send, 4), (share, 3)):
+            pl.when((t >= late) & (t < chunks + late))(functools.partial(stage, t - late))
+        return carry
+
+    lax.fori_loop(0, chunks + 4, step, 0)
+
+    def finish(c, carry):
+        for copy in z_copies(c) + [x_inner(c), x_outer(c), x_relay(c), core_copy(c)]:
+            copy.wait_send()
+        own_copy(c).wait()
+        for r in range(ROUNDS):
+            y_copy(c, r).wait()
+        return carry
+
+    lax.fori_loop(0, chunks, finish, 0)
+
+
+def exchange(records, plan, hops):
+    freqs, part, width = records.shape
+    bands = 8
+    chunks = freqs // bands
+    stations = part * bands
+    block = (stations, width)
+    dma = pltpu.SemaphoreType.DMA
+    return pl.pallas_call(
+        functools.partial(exchange_kernel, hops),
+        out_shape=[
+            jax.ShapeDtypeStruct((chunks,) + block, jnp.bfloat16),
+            jax.ShapeDtypeStruct((ROUNDS, chunks) + block, jnp.bfloat16),
+        ],
+        in_specs=[pl.BlockSpec(memory_space=pltpu.SMEM), pl.BlockSpec(memory_space=pltpu.VMEM)],
+        out_specs=[pl.BlockSpec(memory_space=pl.ANY)] * 2,
+        scratch_shapes=[
+            pltpu.VMEM((chunks, 3, 2, part, width), jnp.bfloat16),
+            pltpu.VMEM((chunks, stations // 2, width), jnp.bfloat16),
+            pltpu.VMEM((chunks, 2, 2) + block, jnp.bfloat16),
+            pltpu.VMEM((ROUNDS, chunks) + block, jnp.bfloat16),
+            dma((chunks, 3, 2)), dma((chunks, 3, 2)), dma((chunks, 3)), dma((chunks, 3)),
+            dma((chunks,)), dma((chunks,)), dma((ROUNDS, chunks)), dma((ROUNDS, chunks)),
+            dma((chunks,)),
+        ],
+        compiler_params=pltpu.CompilerParams(
+            collective_id=1 + hops[0] * 4 + hops[1], has_side_effects=True,
+            vmem_limit_bytes=52 * 1024 * 1024,
+        ),
+        name="exchange_%d%d" % hops,
+    )(plan, records)
 
 
 def body(records, plan):
-    regrouped = lax.all_to_all(records, "freq", split_axis=0, concat_axis=1, tiled=True)
-    values = regrouped.astype(jnp.float32)
-    power_sum = jnp.sum(values * values, -1, keepdims=True) / W
-    white = (values * lax.rsqrt(power_sum + EPS)).astype(jnp.bfloat16)
+    branches = [
+        functools.partial(exchange, hops=(first, second)) for first in range(4) for second in range(4)
+    ]
+    hop = plan // 2 % 4
+    own, got = lax.switch(hop[0] * 4 + hop[1], branches, records, plan)
     me = lax.axis_index("grp")
-    partner = jnp.stack([fetch(white, plan[r]) for r in range(ROUNDS)])
     lower = (me < jnp.bitwise_xor(me, plan)).astype(jnp.int32)
-    within, rounds = spectra(lower, white, partner)
+    within, rounds = spectra(lower, own, got)
     return within, rounds
 
 

time: 283 us -> 155 us (0.55)
  waiting for transfers between devices: 228 us -> 0 us
  Pallas kernels: 16.4 us -> 151 us
  starting transfers between devices: 15.9 us -> 0 us
  other arithmetic: 12 us -> 1.33 us
  local copies, waits for them, and re-layouts: 8.08 us -> 0.58 us
    ppermute x2 -> x0, waiting for transfers between devices: 181 us -> none  [by(): return lambda: lax.ppermute(own, 'grp', [(i, i ^ m) for i in range(N_GRP)])]
    pallas_call x0 -> x1, Pallas kernels: none -> 134 us  [exchange(): pl.pallas_call(functools.partial(exchange_kernel, hops), out_shape=[jax.S...]
    all_to_all x1 -> x0, waiting for transfers between devices: 46.8 us -> none  [body(): lax.all_to_all(records, 'freq', split_axis=0, concat_axis=1, tiled=True)]
    all_to_all x1 -> x0, starting transfers between devices: 8.34 us -> none  [body(): lax.all_to_all(records, 'freq', split_axis=0, concat_axis=1, tiled=True)]
    another operation x1 -> x0, other arithmetic: 7.67 us -> none  [body(): partner = jnp.stack([fetch(white, plan[r]) for r in range(ROUNDS)])]
    ppermute x2 -> x0, starting transfers between devices: 7.56 us -> none  [by(): return lambda: lax.ppermute(own, 'grp', [(i, i ^ m) for i in range(N_GRP)])]
    convert_element_type x1 -> x0, local copies, waits for them, and re-layouts: 3.39 us -> none  [body(): values = regrouped.astype(jnp.float32)]
    reduce_sum x1 -> x0, other arithmetic: 3.06 us -> none  [body(): power_sum = jnp.sum(values * values, -1, keepdims=True) / W]
  transfers between devices with their start and end apart: 3 -> 0, of which waited for: 3 -> 0; matrix products, arithmetic and copies ran while one was open for 0% -> 0% of each run, Pallas kernels for 0% -> 0%
where the time goes in v2:
time: 155 us
  Pallas kernels  151 us (97%)
  between operations  1.94 us (1%)
    pallas_call x1, Pallas kernels, exchange(): pl.pallas_call(functools.partial(exchange_kernel, hops), out_shape=[jax.S...  134 us
    pallas_call x1, Pallas kernels, spectra(): pl.pallas_call(spectra_kernel, grid_spec=pltpu.PrefetchScalarGridSpec(num...  17.1 us

profile of v2, /device:TPU:1, one launch (start us, length us, event | category | flops | bytes accessed | tf_op | source)
XLA Modules:
  0.0 154.9 jit_solution(15928013681766764538)
XLA Ops:
  0.6 0.7 compare_convert_fusion.lower_ref
  1.3 0.7 and_select_fusion
  2.0 0.6 fusion.1
  3.9 134.0 %conditional.1 = ((bf16[8,512,512]{2,1,0:T(8,128)(2,1)}, bf16[2,8,512,512]{3,2,1,0:T(8,128)(2,1)})) conditional(s32[]{:T(128)} %bitcast, (s32[2]{0:T(128)}, bf16[64,64,512]{2,1,0:T(8,128)(2,1)}) %tuple.55, (s32[2]{0:T(128)}, bf16[64,64,512]{2,1,0:T(8,128)(2,1)}) %tuple.55, (s32[2]{0:T(128)}, ...), branch_computations={%region_0.1_spmd, %region_1.2_spmd, %region_2.3_spmd, %region_3.4_... | conditional | bytes 8 | solution.py:275
  3.9 133.7 %exchange_13.1 = (bf16[8,512,512]{2,1,0:T(8,128)(2,1)}, bf16[2,8,512,512]{3,2,1,0:T(8,128)(2,1)}) custom-call(s32[2]{0:T(128)} %get-tuple-element.78.plan_ref, bf16[64,64,512]{2,1,0:T(8,128)(2,1)} %get-tuple-element.79.rec_ref), custom_call_target="tpu_custom_call" | custom-call | tf_op jit(solution)/shard_map/cond/branch_7_fun/exchange_13/pallas_call | solution.py:245
  137.8 17.1 %spectra.1 = (bf16[1,8,10,128,256]{4,3,2,1,0:T(8,128)(2,1)}, bf16[1,2,8,8,128,256]{5,4,3,2,1,0:T(8,128)(2,1)}) custom-call(s32[2]{0:T(128)S(1)} %compare_convert_fusion.lower_ref, bf16[8,512,512]{2,1,0:T(8,128)(2,1)} %get-tuple-element.100.own_ref, bf16[2,8,512,512]{3,2,1,0:T(8,128)(2,1)} %get-tuple-element.101.partner_ref), custom_call_target="tpu_custom_call" | custom-call | flops 7000000000 | bytes 27000000 | tf_op jit(solution)/shard_map/spectra/pallas_call | solution.py:59

commit v3 on v2

v3 whole, which is shorter than its diff:
```python
import functools

import jax
import jax.numpy as jnp
from jax import lax
from jax.experimental import pallas as pl
from jax.experimental.pallas import tpu as pltpu
from jax.sharding import PartitionSpec as P

GSTA = 128
W = 256
GPD = 4
ROUNDS = 2
N_GRP = 16
EPS = 1e-06


def turned(block):
    return jnp.concatenate([-block[:, W:], block[:, :W]], -1)


def times(left, right):
    return lax.dot_general(left, right, (((1,), (1,)), ((), ())), preferred_element_type=jnp.float32)


def spectra_kernel(plan_ref, own_ref, partner_ref, within_ref, round_ref):
    own = own_ref.at[0]
    me = lax.axis_index("grp")

    def cross(rows, right_ref, start):
        right = right_ref[pl.ds(start, GSTA), :]
        packed = jnp.concatenate([right, turned(right)], 0)
        return (times(own[pl.ds(0, rows), :], packed) * W ** (-0.5)).astype(jnp.bfloat16)

    pairs = [(i, j) for i in range(GPD) for j in range(i, GPD)]
    for j in range(GPD):
        product = cross((j + 1) * GSTA, own, j * GSTA)
        for i in range(j + 1):
            within_ref[0, 0, pairs.index((i, j))] = product[i * GSTA : (i + 1) * GSTA]
    for r in range(ROUNDS):
        partner = partner_ref.at[r, 0]
        lower = me < jnp.bitwise_xor(me, plan_ref[r])

        @pl.when(lower)
        def _():
            for j in range(GPD):
                product = cross(2 * GSTA, partner, j * GSTA)
                for i in range(2):
                    round_ref[0, r, 0, i * GPD + j] = product[i * GSTA : (i + 1) * GSTA]

        @pl.when(jnp.logical_not(lower))
        def _():
            for j in range(2):
                product = cross(GPD * GSTA, partner, (2 + j) * GSTA)
                for i in range(GPD):
                    round_ref[0, r, 0, i * 2 + j] = product[i * GSTA : (i + 1) * GSTA]


def spectra(plan, own, partner):
    freqs, stations, width = own.shape
    return pl.pallas_call(
        spectra_kernel,
        grid_spec=pltpu.PrefetchScalarGridSpec(
            num_scalar_prefetch=1,
            grid=(freqs,),
            in_specs=[
                pl.BlockSpec((1, stations, width), lambda f, _: (f, 0, 0)),
                pl.BlockSpec((ROUNDS, 1, stations, width), lambda f, _: (0, f, 0, 0)),
            ],
            out_specs=[
                pl.BlockSpec((1, 1, 10, GSTA, 2 * GSTA), lambda f, _: (0, f, 0, 0, 0)),
                pl.BlockSpec((1, ROUNDS, 1, 8, GSTA, 2 * GSTA), lambda f, _: (0, 0, f, 0, 0, 0)),
            ],
        ),
        out_shape=[
            jax.ShapeDtypeStruct((1, freqs, 10, GSTA, 2 * GSTA), jnp.bfloat16),
            jax.ShapeDtypeStruct((1, ROUNDS, freqs, 8, GSTA, 2 * GSTA), jnp.bfloat16),
        ],
        compiler_params=pltpu.CompilerParams(vmem_limit_bytes=48 * 1024 * 1024),
        cost_estimate=pl.CostEstimate(flops=7 * 10**9, bytes_accessed=27 * 10**6, transcendentals=0),
        name="spectra",
    )(plan, own, partner)

X_LO = 8
X_HI = 4
BANDS = 8
SLICES = 2


def flip(index, size):
    return index + size - 2 * size * (index // size % 2)


def meet(index, bits, size):
    for bit in (1, 2):
        if bits & bit:
            index = flip(index, size * bit)
    return index


def exchange_kernel(
    hops, pass_on, plan_ref, rec_ref, own_ref, got_ref, raw, ready, across, blocks, picked,
    raw_sem, z_out, z_in, x_out, x_in, core_out, core_in, y_out, y_in, own_sem,
):
    chunks = blocks.shape[0]
    half = BANDS // 2
    g = lax.axis_index("grp")
    q = lax.axis_index("freq")
    z = q % 4
    hi = q // X_HI
    inner = (flip(g, X_LO), q)
    outer = (flip(g, X_LO), flip(q, X_HI))
    mate = (flip(g, 1), q)
    aside = [(g, meet(q, j, 1)) for j in range(1, 4)]
    along = [(meet(g, hop, 2), q) for hop in hops]
    sends = [r for r in range(ROUNDS) if not (pass_on and pass_on[1] == r)]
    friends = [inner, outer, mate] + aside + [along[r] for r in sends if hops[r]]
    if pass_on:
        first, second, turn, swap = pass_on
        onward = (meet(flip(g, 1) if swap else g, turn, 2), q)
        friends.append(onward)

    def raw_copy(c):
        return pltpu.make_async_copy(rec_ref.at[:, c], raw.at[c], raw_sem.at[c])

    def load(c, carry):
        raw_copy(c).start()
        return carry

    lax.fori_loop(0, chunks, load, 0)

    barrier = pltpu.get_barrier_semaphore()
    for friend in friends:
        pl.semaphore_signal(barrier, inc=1, device_id=friend, device_id_type=pl.DeviceIdType.MESH)
    pl.semaphore_wait(barrier, len(friends))

    near = pl.ds(hi * half, half)
    far = pl.ds((1 - hi) * half, half)

    def remote(source, target, sent, landed, device):
        return pltpu.make_async_remote_copy(
            src_ref=source, dst_ref=target, send_sem=sent, recv_sem=landed,
            device_id=device, device_id_type=pl.DeviceIdType.MESH,
        )

    def z_copies(c):
        copies = []
        for j in range(3):
            copies.append(remote(
                ready.at[c, j, 0], blocks.at[c, 0, 0, hi * half + z],
                z_out.at[c, j, 0], z_in.at[c, j, 0], aside[j],
            ))
            copies.append(remote(
                ready.at[c, j, 1], across.at[c, z],
                z_out.at[c, j, 1], z_in.at[c, j, 1], aside[j],
            ))
        return copies

    def x_inner(c):
        return remote(
            blocks.at[c, 0, 0, near], blocks.at[c, 0, 1, near], x_out.at[c, 0], x_in.at[c, 0], inner
        )

    def x_outer(c, rows):
        return remote(across.at[c], blocks.at[c, 0, 1, rows], x_out.at[c, 1], x_in.at[c, 1], outer)

    def x_relay(c):
        return remote(
            blocks.at[c, 0, 1, far], blocks.at[c, 0, 0, far], x_out.at[c, 2], x_in.at[c, 2], inner
        )

    def core_copy(c):
        return remote(blocks.at[c, 0], blocks.at[c, 1], core_out.at[c], core_in.at[c], mate)

    def own_copy(c):
        return pltpu.make_async_copy(
            blocks.at[c, 0, 0], own_ref.at[c // SLICES, :, c % SLICES], own_sem.at[c]
        )

    def landing(c, r):
        return got_ref.at[r, c // SLICES, :, c % SLICES]

    def y_copy(c, r):
        if hops[r]:
            return remote(
                picked.at[r, c], landing(c, r), y_out.at[r, c], y_in.at[r, c], along[r]
            )
        return pltpu.make_async_copy(picked.at[r, c], landing(c, r), y_out.at[r, c])

    def onward_copy(c):
        return remote(
            landing(c, first), landing(c, second), y_out.at[second, c], y_in.at[second, c], onward
        )

    def whiten(c):
        raw_copy(c).wait()
        for j in range(4):
            for k in range(2):
                band = (hi if k == 0 else 1 - hi) * half + meet(z, j, 1)
                values = raw[c, band].astype(jnp.float32)
                power = jnp.sum(values * values, -1, keepdims=True) / W
                white = (values * lax.rsqrt(power + EPS)).astype(jnp.bfloat16)
                if j:
                    ready[c, j - 1, k] = white
                elif k:
                    across[c, z] = white
                else:
                    blocks[c, 0, 0, hi * half + z] = white
        for copy in z_copies(c):
            copy.start()

    def spread(c):
        for copy in z_copies(c):
            copy.wait_recv()
        x_inner(c).start()
        x_outer(c, near).start()

    def relay(c):
        x_outer(c, far).wait_recv()
        x_relay(c).start()

    def share(c):
        x_inner(c).wait_recv()
        x_relay(c).wait_recv()
        core_copy(c).start()
        own_copy(c).start()

    def send(c):
        core_copy(c).wait_recv()
        for r in sends:
            other_lo = plan_ref[r] >= X_LO
            other_core = plan_ref[r] % 2 == 1
            here = jnp.where(other_lo, blocks[c, 0, 1], blocks[c, 0, 0])
            there = jnp.where(other_lo, blocks[c, 1, 1], blocks[c, 1, 0])
            picked[r, c] = jnp.where(other_core, there, here)
            y_copy(c, r).start()

    def hand_on(c):
        y_copy(c, first).wait_recv()
        onward_copy(c).start()

    stages = [(spread, 1), (whiten, 0), (relay, 2), (send, 4), (share, 3)]
    if pass_on:
        stages.append((hand_on, 6))

    def step(t, carry):
        for stage, late in stages:
            pl.when((t >= late) & (t < chunks + late))(functools.partial(stage, t - late))
        return carry

    lax.fori_loop(0, chunks + max(late for _, late in stages), step, 0)

    def finish(c, carry):
        for copy in z_copies(c) + [x_inner(c), x_outer(c, near), x_relay(c), core_copy(c)]:
            copy.wait_send()
        own_copy(c).wait()
        for r in sends:
            if pass_on and r == first:
                y_copy(c, r).wait_send()
            else:
                y_copy(c, r).wait()
        if pass_on:
            onward_copy(c).wait()
        return carry

    lax.fori_loop(0, chunks, finish, 0)


def exchange(records, plan, variant, number):
    freqs, stations, width = records.shape
    chunks = freqs // BANDS * SLICES
    part = (stations // SLICES, width)
    block = (BANDS,) + part
    dma = pltpu.SemaphoreType.DMA
    own, got = pl.pallas_call(
        functools.partial(exchange_kernel, *variant),
        out_shape=[
            jax.ShapeDtypeStruct((freqs // BANDS, BANDS, SLICES) + part, jnp.bfloat16),
            jax.ShapeDtypeStruct((ROUNDS, freqs // BANDS, BANDS, SLICES) + part, jnp.bfloat16),
        ],
        in_specs=[pl.BlockSpec(memory_space=pltpu.SMEM), pl.BlockSpec(memory_space=pl.ANY)],
        out_specs=[pl.BlockSpec(memory_space=pl.ANY)] * 2,
        scratch_shapes=[
            pltpu.VMEM((chunks,) + block, jnp.bfloat16),
            pltpu.VMEM((chunks, 3, 2) + part, jnp.bfloat16),
            pltpu.VMEM((chunks, BANDS // 2) + part, jnp.bfloat16),
            pltpu.VMEM((chunks, 2, 2) + block, jnp.bfloat16),
            pltpu.VMEM((ROUNDS, chunks) + block, jnp.bfloat16),
            dma((chunks,)),
            dma((chunks, 3, 2)), dma((chunks, 3, 2)), dma((chunks, 3)), dma((chunks, 3)),
            dma((chunks,)), dma((chunks,)), dma((ROUNDS, chunks)), dma((ROUNDS, chunks)),
            dma((chunks,)),
        ],
        compiler_params=pltpu.CompilerParams(
            collective_id=1 + number, has_side_effects=True, vmem_limit_bytes=52 * 1024 * 1024
        ),
        name="exchange_%d" % number,
    )(plan, records.reshape((BANDS, chunks) + part))
    shape = (freqs // BANDS, stations * BANDS, width)
    return own.reshape(shape), got.reshape((ROUNDS,) + shape)


def variants():
    found = [((first, second), None) for first in range(4) for second in range(4)]
    found += [((hop, hop), (0, 1, 0, 1)) for hop in (1, 2, 3)]
    for swap in range(2):
        for first, second in ((1, 2), (2, 1), (2, 3), (3, 2)):
            order = (1, 0) if first == 2 else (0, 1)
            odd = second if first == 2 else first
            found.append(((first, second), order + (2 ^ odd, swap)))
    return found


def variant_number(plan):
    first, second = plan[0] >> 1 & 3, plan[1] >> 1 & 3
    change = plan[0] ^ plan[1]
    both = first * second
    direct = (first << 2) + second
    turned_off = 19 + ((change & 1) << 2) + jnp.minimum((direct >> 1) - 3, 3)
    relayed = jnp.where(first == second, 15 + first, turned_off)
    return jnp.where((change < X_LO) & (both != 0) & (both != 3), relayed, direct)


def body(records, plan):
    branches = [
        functools.partial(exchange, variant=variant, number=number)
        for number, variant in enumerate(variants())
    ]
    own, got = lax.switch(variant_number(plan), branches, records, plan)
    return spectra(plan, own, got)


def solution(mesh):
    placed = (P(None, ("grp", "freq"), None), P())
    return jax.shard_map(
        body,
        mesh=mesh,
        in_specs=placed,
        out_specs=(P("grp", "freq", None, None, None), P("grp", None, "freq", None, None, None)),
        check_vma=False,
    )
```

time: 155 us -> 233 us (1.50)
  Pallas kernels: 151 us -> 226 us
    pallas_call x1, Pallas kernels: 134 us -> 210 us  [exchange(): pl.pallas_call(functools.partial(exchange_kernel, *variant), out_shape=[j...]
where the time goes in v3:
time: 233 us; the launch traced here: 231 us
  Pallas kernels  226 us (97%)
  between operations  3.25 us (1%)
    pallas_call x1, Pallas kernels, exchange(): pl.pallas_call(functools.partial(exchange_kernel, *variant), out_shape=[j...  210 us
    pallas_call x1, Pallas kernels, spectra(): pl.pallas_call(spectra_kernel, grid_spec=pltpu.PrefetchScalarGridSpec(num...  15.7 us

profile of v3, /device:TPU:1, one launch (start us, length us, event | category | flops | bytes accessed | tf_op | source)
XLA Modules:
  0.0 231.1 jit_solution(191377189719876061)
XLA Ops:
  0.6 1.3 fusion
  4.6 210.8 %conditional.1 = (bf16[8,512,512]{2,1,0:T(8,128)(2,1)}, bf16[2,8,512,512]{3,2,1,0:T(8,128)(2,1)S(1)}) conditional(s32[]{:T(128)} %clamp.3, (bf16[64,64,512]{2,1,0:T(8,128)(2,1)}, s32[2]{0:T(128)}) %tuple.115, (bf16[64,64,512]{2,1,0:T(8,128)(2,1)}, s32[2]{0:T(128)}) %tuple.115, (bf16[64,64,512]{2,1,0:T(8,128)(2,1)}, ...), branch_computations={%region_0.1_spmd, %region_1.2_spmd, %region_2.3_spmd, %region_3.4_... | conditional | bytes 16 | solution.py:329
  4.8 210.2 %exchange_15.1 = (bf16[8,8,2,32,512]{4,3,2,1,0:T(8,128)(2,1)}, bf16[2,8,8,2,32,512]{5,4,3,2,1,0:T(8,128)(2,1)S(1)}) custom-call(s32[2]{0:T(128)} %get-tuple-element.168.plan_ref, bf16[8,16,32,512]{3,2,1,0:T(8,128)(2,1)} %bitcast.100), custom_call_target="tpu_custom_call" | custom-call | tf_op jit(solution)/shard_map/cond/branch_15_fun/exchange_15/pallas_call | solution.py:275
  215.4 15.7 %spectra.1 = (bf16[1,8,10,128,256]{4,3,2,1,0:T(8,128)(2,1)}, bf16[1,2,8,8,128,256]{5,4,3,2,1,0:T(8,128)(2,1)}) custom-call(s32[2]{0:T(128)} %plan_ref.1, bf16[8,512,512]{2,1,0:T(8,128)(2,1)} %get-tuple-element.220.own_ref, bf16[2,8,512,512]{3,2,1,0:T(8,128)(2,1)S(1)} %get-tuple-element.221.partner_ref), custom_call_target="tpu_custom_call" | custom-call | flops 7000000000 | bytes 27000000 | tf_op jit(solution)/shard_map/spectra/pallas_call | solution.py:61

commit v4 on v3

--- a/solution.py
+++ b/solution.py
@@ -23,41 +23,50 @@
     return lax.dot_general(left, right, (((1,), (1,)), ((), ())), preferred_element_type=jnp.float32)
 
 
-def spectra_kernel(plan_ref, own_ref, partner_ref, within_ref, round_ref):
+def group_pairs():
+    return [(i, j) for i in range(GPD) for j in range(i, GPD)]
+
+
+def cross(left, right):
+    packed = jnp.concatenate([right, turned(right)], 0)
+    return (times(left, packed) * W ** (-0.5)).astype(jnp.bfloat16)
+
+
+def hop_of(mask):
+    return mask >> 1 & 3
+
+
+def swapped_slots(plan):
+    return (hop_of(plan[0]) > hop_of(plan[1])).astype(jnp.int32)
+
+
+def spectra_kernel(plan_ref, own_ref, partner_ref, inside_ref, within_ref, round_ref):
     own = own_ref.at[0]
     me = lax.axis_index("grp")
-
-    def cross(rows, right_ref, start):
-        right = right_ref[pl.ds(start, GSTA), :]
-        packed = jnp.concatenate([right, turned(right)], 0)
-        return (times(own[pl.ds(0, rows), :], packed) * W ** (-0.5)).astype(jnp.bfloat16)
-
-    pairs = [(i, j) for i in range(GPD) for j in range(i, GPD)]
-    for j in range(GPD):
-        product = cross((j + 1) * GSTA, own, j * GSTA)
-        for i in range(j + 1):
-            within_ref[0, 0, pairs.index((i, j))] = product[i * GSTA : (i + 1) * GSTA]
+    swapped = swapped_slots(plan_ref)
+    within_ref[0] = inside_ref[...]
     for r in range(ROUNDS):
-        partner = partner_ref.at[r, 0]
+        partner = partner_ref.at[swapped if r == 0 else 1 - swapped, 0]
         lower = me < jnp.bitwise_xor(me, plan_ref[r])
 
         @pl.when(lower)
         def _():
             for j in range(GPD):
-                product = cross(2 * GSTA, partner, j * GSTA)
+                product = cross(own[pl.ds(0, 2 * GSTA), :], partner[pl.ds(j * GSTA, GSTA), :])
                 for i in range(2):
                     round_ref[0, r, 0, i * GPD + j] = product[i * GSTA : (i + 1) * GSTA]
 
         @pl.when(jnp.logical_not(lower))
         def _():
             for j in range(2):
-                product = cross(GPD * GSTA, partner, (2 + j) * GSTA)
+                product = cross(own[...], partner[pl.ds((2 + j) * GSTA, GSTA), :])
                 for i in range(GPD):
                     round_ref[0, r, 0, i * 2 + j] = product[i * GSTA : (i + 1) * GSTA]
 
 
-def spectra(plan, own, partner):
+def spectra(plan, own, partner, inside):
     freqs, stations, width = own.shape
+    pairs = inside.shape[1:]
     return pl.pallas_call(
         spectra_kernel,
         grid_spec=pltpu.PrefetchScalarGridSpec(
@@ -66,20 +75,22 @@
             in_specs=[
                 pl.BlockSpec((1, stations, width), lambda f, _: (f, 0, 0)),
                 pl.BlockSpec((ROUNDS, 1, stations, width), lambda f, _: (0, f, 0, 0)),
+                pl.BlockSpec((1,) + pairs, lambda f, _: (f, 0, 0, 0)),
             ],
             out_specs=[
-                pl.BlockSpec((1, 1, 10, GSTA, 2 * GSTA), lambda f, _: (0, f, 0, 0, 0)),
+                pl.BlockSpec((1, 1) + pairs, lambda f, _: (0, f, 0, 0, 0)),
                 pl.BlockSpec((1, ROUNDS, 1, 8, GSTA, 2 * GSTA), lambda f, _: (0, 0, f, 0, 0, 0)),
             ],
         ),
         out_shape=[
-            jax.ShapeDtypeStruct((1, freqs, 10, GSTA, 2 * GSTA), jnp.bfloat16),
+            jax.ShapeDtypeStruct((1, freqs) + pairs, jnp.bfloat16),
             jax.ShapeDtypeStruct((1, ROUNDS, freqs, 8, GSTA, 2 * GSTA), jnp.bfloat16),
         ],
-        compiler_params=pltpu.CompilerParams(vmem_limit_bytes=48 * 1024 * 1024),
-        cost_estimate=pl.CostEstimate(flops=7 * 10**9, bytes_accessed=27 * 10**6, transcendentals=0),
+        compiler_params=pltpu.CompilerParams(vmem_limit_bytes=32 * 1024 * 1024),
+        cost_estimate=pl.CostEstimate(flops=5 * 10**9, bytes_accessed=32 * 10**6, transcendentals=0),
         name="spectra",
-    )(plan, own, partner)
+    )(plan, own, partner, inside)
+
 
 X_LO = 8
 X_HI = 4
@@ -99,10 +110,13 @@
 
 
 def exchange_kernel(
-    hops, pass_on, plan_ref, rec_ref, own_ref, got_ref, raw, ready, across, blocks, picked,
-    raw_sem, z_out, z_in, x_out, x_in, core_out, core_in, y_out, y_in, own_sem,
+    hops, pass_on, plan_ref, rec_ref, own_ref, got_ref, inside_ref,
+    raw, ready, across, blocks, picked, mine, inside,
+    raw_sem, z_out, z_in, x_out, x_in, core_out, core_in, y_out, y_in, own_sem, inside_sem,
 ):
     chunks = blocks.shape[0]
+    swapped = swapped_slots(plan_ref)
+    masks = [plan_ref[swapped], plan_ref[1 - swapped]]
     half = BANDS // 2
     g = lax.axis_index("grp")
     q = lax.axis_index("freq")
@@ -228,8 +242,8 @@
     def send(c):
         core_copy(c).wait_recv()
         for r in sends:
-            other_lo = plan_ref[r] >= X_LO
-            other_core = plan_ref[r] % 2 == 1
+            other_lo = masks[r] >= X_LO
+            other_core = masks[r] % 2 == 1
             here = jnp.where(other_lo, blocks[c, 0, 1], blocks[c, 0, 0])
             there = jnp.where(other_lo, blocks[c, 1, 1], blocks[c, 1, 0])
             picked[r, c] = jnp.where(other_core, there, here)
@@ -239,13 +253,34 @@
         y_copy(c, first).wait_recv()
         onward_copy(c).start()
 
-    stages = [(spread, 1), (whiten, 0), (relay, 2), (send, 4), (share, 3)]
+    def inside_copy(f):
+        return pltpu.make_async_copy(inside.at[f], inside_ref.at[f], inside_sem.at[f])
+
+    def pair_up(c):
+        f = c // SLICES
+        part = blocks.shape[-2]
+        for p in range(BANDS):
+            for piece in range(SLICES):
+                start = (p * SLICES + piece) * part
+                mine[start : start + part] = blocks[f * SLICES + piece, 0, 0, p]
+        pairs = group_pairs()
+        for j in range(GPD):
+            product = cross(mine[: (j + 1) * GSTA], mine[j * GSTA : (j + 1) * GSTA])
+            for i in range(j + 1):
+                inside[f, pairs.index((i, j))] = product[i * GSTA : (i + 1) * GSTA]
+        inside_copy(f).start()
+
+    stages = [(whiten, 0), (spread, 1), (relay, 2), (share, 3), (send, 3)]
     if pass_on:
-        stages.append((hand_on, 6))
+        stages.append((hand_on, 5))
 
     def step(t, carry):
         for stage, late in stages:
             pl.when((t >= late) & (t < chunks + late))(functools.partial(stage, t - late))
+        done = t - 3
+        pl.when((done >= 0) & (done < chunks) & (done % SLICES == SLICES - 1))(
+            functools.partial(pair_up, done)
+        )
         return carry
 
     lax.fori_loop(0, chunks + max(late for _, late in stages), step, 0)
@@ -254,6 +289,7 @@
         for copy in z_copies(c) + [x_inner(c), x_outer(c, near), x_relay(c), core_copy(c)]:
             copy.wait_send()
         own_copy(c).wait()
+        pl.when(c % SLICES == 0)(lambda: inside_copy(c // SLICES).wait())
         for r in sends:
             if pass_on and r == first:
                 y_copy(c, r).wait_send()
@@ -272,53 +308,54 @@
     part = (stations // SLICES, width)
     block = (BANDS,) + part
     dma = pltpu.SemaphoreType.DMA
-    own, got = pl.pallas_call(
+    pairs = (len(group_pairs()), GSTA, 2 * GSTA)
+    own, got, inside = pl.pallas_call(
         functools.partial(exchange_kernel, *variant),
         out_shape=[
             jax.ShapeDtypeStruct((freqs // BANDS, BANDS, SLICES) + part, jnp.bfloat16),
             jax.ShapeDtypeStruct((ROUNDS, freqs // BANDS, BANDS, SLICES) + part, jnp.bfloat16),
+            jax.ShapeDtypeStruct((freqs // BANDS,) + pairs, jnp.bfloat16),
         ],
         in_specs=[pl.BlockSpec(memory_space=pltpu.SMEM), pl.BlockSpec(memory_space=pl.ANY)],
-        out_specs=[pl.BlockSpec(memory_space=pl.ANY)] * 2,
+        out_specs=[pl.BlockSpec(memory_space=pl.ANY)] * 3,
         scratch_shapes=[
             pltpu.VMEM((chunks,) + block, jnp.bfloat16),
             pltpu.VMEM((chunks, 3, 2) + part, jnp.bfloat16),
             pltpu.VMEM((chunks, BANDS // 2) + part, jnp.bfloat16),
             pltpu.VMEM((chunks, 2, 2) + block, jnp.bfloat16),
             pltpu.VMEM((ROUNDS, chunks) + block, jnp.bfloat16),
+            pltpu.VMEM((stations * BANDS, width), jnp.bfloat16),
+            pltpu.VMEM((freqs // BANDS,) + pairs, jnp.bfloat16),
             dma((chunks,)),
             dma((chunks, 3, 2)), dma((chunks, 3, 2)), dma((chunks, 3)), dma((chunks, 3)),
             dma((chunks,)), dma((chunks,)), dma((ROUNDS, chunks)), dma((ROUNDS, chunks)),
-            dma((chunks,)),
+            dma((chunks,)), dma((freqs // BANDS,)),
         ],
         compiler_params=pltpu.CompilerParams(
-            collective_id=1 + number, has_side_effects=True, vmem_limit_bytes=52 * 1024 * 1024
+            collective_id=1 + number, has_side_effects=True, vmem_limit_bytes=46 * 1024 * 1024
         ),
         name="exchange_%d" % number,
     )(plan, records.reshape((BANDS, chunks) + part))
     shape = (freqs // BANDS, stations * BANDS, width)
-    return own.reshape(shape), got.reshape((ROUNDS,) + shape)
+    return own.reshape(shape), got.reshape((ROUNDS,) + shape), inside
 
 
 def variants():
-    found = [((first, second), None) for first in range(4) for second in range(4)]
+    found = [((low, high), None) for high in range(4) for low in range(high + 1)]
     found += [((hop, hop), (0, 1, 0, 1)) for hop in (1, 2, 3)]
-    for swap in range(2):
-        for first, second in ((1, 2), (2, 1), (2, 3), (3, 2)):
-            order = (1, 0) if first == 2 else (0, 1)
-            odd = second if first == 2 else first
-            found.append(((first, second), order + (2 ^ odd, swap)))
+    found += [((1, 2), (0, 1, 3, swap)) for swap in range(2)]
+    found += [((2, 3), (1, 0, 1, swap)) for swap in range(2)]
     return found
 
 
 def variant_number(plan):
-    first, second = plan[0] >> 1 & 3, plan[1] >> 1 & 3
+    first, second = hop_of(plan[0]), hop_of(plan[1])
+    low, high = jnp.minimum(first, second), jnp.maximum(first, second)
     change = plan[0] ^ plan[1]
-    both = first * second
-    direct = (first << 2) + second
-    turned_off = 19 + ((change & 1) << 2) + jnp.minimum((direct >> 1) - 3, 3)
-    relayed = jnp.where(first == second, 15 + first, turned_off)
-    return jnp.where((change < X_LO) & (both != 0) & (both != 3), relayed, direct)
+    direct = (high * (high + 1) >> 1) + low
+    turned_off = 13 + ((high & 1) << 1) + (change & 1)
+    relayed = jnp.where(low == high, 9 + high, turned_off)
+    return jnp.where((change < X_LO) & (low != 0) & (low * high != 3), relayed, direct)
 
 
 def body(records, plan):
@@ -326,8 +363,7 @@
         functools.partial(exchange, variant=variant, number=number)
         for number, variant in enumerate(variants())
     ]
-    own, got = lax.switch(variant_number(plan), branches, records, plan)
-    return spectra(plan, own, got)
+    return spectra(plan, *lax.switch(variant_number(plan), branches, records, plan))
 
 
 def solution(mesh):

time: 233 us -> 147 us (0.63)
  Pallas kernels: 226 us -> 141 us
    pallas_call x1, Pallas kernels: 210 us -> 131 us  [exchange(): pl.pallas_call(functools.partial(exchange_kernel, *variant), out_shape=[j...]
    pallas_call x1, Pallas kernels: 15.7 us -> 10.8 us  [spectra(): pl.pallas_call(spectra_kernel, grid_spec=pltpu.PrefetchScalarGridSpec(num...]
where the time goes in v4:
time: 147 us
  Pallas kernels  141 us (96%)
  between operations  3.26 us (2%)
    pallas_call x1, Pallas kernels, exchange(): pl.pallas_call(functools.partial(exchange_kernel, *variant), out_shape=[j...  131 us
    pallas_call x1, Pallas kernels, spectra(): pl.pallas_call(spectra_kernel, grid_spec=pltpu.PrefetchScalarGridSpec(num...  10.8 us

profile of v4, /device:TPU:1, one launch (start us, length us, event | category | flops | bytes accessed | tf_op | source)
XLA Modules:
  0.0 146.8 jit_solution(773114059373170696)
XLA Ops:
  0.6 1.3 fusion
  4.6 131.5 %conditional.1 = (bf16[8,512,512]{2,1,0:T(8,128)(2,1)S(1)}, bf16[2,8,512,512]{3,2,1,0:T(8,128)(2,1)S(1)}, bf16[8,10,128,256]{3,2,1,0:T(8,128)(2,1)S(1)}) conditional(s32[]{:T(128)} %clamp.3, (bf16[64,64,512]{2,1,0:T(8,128)(2,1)}, s32[2]{0:T(128)}) %tuple.75, (bf16[64,64,512]{2,1,0:T(8,128)(2,1)}, ...), branch_computations={%region_0.1_spmd, %region_1.2_spmd, %region_2.3_spmd, %region_3.4_... | conditional | bytes 24 | solution.py:366
  5.1 130.6 %exchange_16.1 = (bf16[8,8,2,32,512]{4,3,2,1,0:T(8,128)(2,1)S(1)}, bf16[2,8,8,2,32,512]{5,4,3,2,1,0:T(8,128)(2,1)S(1)}, bf16[8,10,128,256]{3,2,1,0:T(8,128)(2,1)S(1)}) custom-call(s32[2]{0:T(128)} %get-tuple-element.148.plan_ref, bf16[8,16,32,512]{3,2,1,0:T(8,128)(2,1)} %bitcast.71), custom_call_target="tpu_custom_call" | custom-call | tf_op jit(solution)/shard_map/cond/branch_16_fun/exchange_16/pallas_call | solution.py:312
  136.1 10.8 %spectra.1 = (bf16[1,8,10,128,256]{4,3,2,1,0:T(8,128)(2,1)}, bf16[1,2,8,8,128,256]{5,4,3,2,1,0:T(8,128)(2,1)}) custom-call(s32[2]{0:T(128)} %plan_ref.1, bf16[8,512,512]{2,1,0:T(8,128)(2,1)S(1)} %get-tuple-element.158.own_ref, bf16[2,8,512,512]{3,2,1,0:T(8,128)(2,1)S(1)} %get-tuple-element.159.partner_ref, ...), custom_call_target="tpu_custom_call" | custom-call | flops 5000000000 | bytes 32000000 | tf_op jit(solution)/shard_map/spectra/pallas_call | solution.py:70

commit v5 on v4

--- a/solution.py
+++ b/solution.py
@@ -40,56 +40,68 @@
     return (hop_of(plan[0]) > hop_of(plan[1])).astype(jnp.int32)
 
 
-def spectra_kernel(plan_ref, own_ref, partner_ref, inside_ref, within_ref, round_ref):
-    own = own_ref.at[0]
+def spectra_kernel(
+    plan_ref, own_ref, got_ref, inside_ref, within_ref, round_ref, staged, within_sem, round_sem
+):
+    freqs = own_ref.shape[0]
     me = lax.axis_index("grp")
     swapped = swapped_slots(plan_ref)
-    within_ref[0] = inside_ref[...]
-    for r in range(ROUNDS):
-        partner = partner_ref.at[swapped if r == 0 else 1 - swapped, 0]
-        lower = me < jnp.bitwise_xor(me, plan_ref[r])
-
-        @pl.when(lower)
-        def _():
-            for j in range(GPD):
-                product = cross(own[pl.ds(0, 2 * GSTA), :], partner[pl.ds(j * GSTA, GSTA), :])
-                for i in range(2):
-                    round_ref[0, r, 0, i * GPD + j] = product[i * GSTA : (i + 1) * GSTA]
-
-        @pl.when(jnp.logical_not(lower))
-        def _():
-            for j in range(2):
-                product = cross(own[...], partner[pl.ds((2 + j) * GSTA, GSTA), :])
-                for i in range(GPD):
-                    round_ref[0, r, 0, i * 2 + j] = product[i * GSTA : (i + 1) * GSTA]
-
-
-def spectra(plan, own, partner, inside):
-    freqs, stations, width = own.shape
-    pairs = inside.shape[1:]
+    within_copy = pltpu.make_async_copy(inside_ref, within_ref.at[0], within_sem)
+    within_copy.start()
+
+    def round_copy(f, r):
+        return pltpu.make_async_copy(staged.at[r, f], round_ref.at[0, r, f], round_sem.at[r, f])
+
+    def make(f, carry):
+        own = own_ref.at[f]
+        for r in range(ROUNDS):
+            partner = got_ref.at[swapped if r == 0 else 1 - swapped, f]
+            lower = me < jnp.bitwise_xor(me, plan_ref[r])
+
+            @pl.when(lower)
+            def _():
+                for j in range(GPD):
+                    product = cross(own[pl.ds(0, 2 * GSTA), :], partner[pl.ds(j * GSTA, GSTA), :])
+                    for i in range(2):
+                        staged[r, f, i * GPD + j] = product[i * GSTA : (i + 1) * GSTA]
+
+            @pl.when(jnp.logical_not(lower))
+            def _():
+                for j in range(2):
+                    product = cross(own[...], partner[pl.ds((2 + j) * GSTA, GSTA), :])
+                    for i in range(GPD):
+                        staged[r, f, i * 2 + j] = product[i * GSTA : (i + 1) * GSTA]
+
+            round_copy(f, r).start()
+        return carry
+
+    def finish(f, carry):
+        for r in range(ROUNDS):
+            round_copy(f, r).wait()
+        return carry
+
+    lax.fori_loop(0, freqs, make, 0)
+    lax.fori_loop(0, freqs, finish, 0)
+    within_copy.wait()
+
+
+def spectra(plan, own, got, inside):
+    freqs = own.shape[0]
+    rounds = (ROUNDS, freqs, 8, GSTA, 2 * GSTA)
+    dma = pltpu.SemaphoreType.DMA
     return pl.pallas_call(
         spectra_kernel,
-        grid_spec=pltpu.PrefetchScalarGridSpec(
-            num_scalar_prefetch=1,
-            grid=(freqs,),
-            in_specs=[
-                pl.BlockSpec((1, stations, width), lambda f, _: (f, 0, 0)),
-                pl.BlockSpec((ROUNDS, 1, stations, width), lambda f, _: (0, f, 0, 0)),
-                pl.BlockSpec((1,) + pairs, lambda f, _: (f, 0, 0, 0)),
-            ],
-            out_specs=[
-                pl.BlockSpec((1, 1) + pairs, lambda f, _: (0, f, 0, 0, 0)),
-                pl.BlockSpec((1, ROUNDS, 1, 8, GSTA, 2 * GSTA), lambda f, _: (0, 0, f, 0, 0, 0)),
-            ],
-        ),
+        in_specs=[pl.BlockSpec(memory_space=pltpu.SMEM)] + [pl.BlockSpec(memory_space=pltpu.VMEM)] * 3,
+        out_specs=[pl.BlockSpec(memory_space=pl.ANY)] * 2,
         out_shape=[
-            jax.ShapeDtypeStruct((1, freqs) + pairs, jnp.bfloat16),
-            jax.ShapeDtypeStruct((1, ROUNDS, freqs, 8, GSTA, 2 * GSTA), jnp.bfloat16),
+            jax.ShapeDtypeStruct((1,) + inside.shape, jnp.bfloat16),
+            jax.ShapeDtypeStruct((1,) + rounds, jnp.bfloat16),
         ],
-        compiler_params=pltpu.CompilerParams(vmem_limit_bytes=32 * 1024 * 1024),
-        cost_estimate=pl.CostEstimate(flops=5 * 10**9, bytes_accessed=32 * 10**6, transcendentals=0),
+        scratch_shapes=[pltpu.VMEM(rounds, jnp.bfloat16), dma, dma((ROUNDS, freqs))],
+        compiler_params=pltpu.CompilerParams(vmem_limit_bytes=36 * 1024 * 1024),
+        cost_estimate=pl.CostEstimate(flops=5 * 10**9, bytes_accessed=14 * 10**6, transcendentals=0),
         name="spectra",
-    )(plan, own, partner, inside)
+    )(plan, own, got, inside)
 
 
 X_LO = 8
@@ -270,7 +282,7 @@
                 inside[f, pairs.index((i, j))] = product[i * GSTA : (i + 1) * GSTA]
         inside_copy(f).start()
 
-    stages = [(whiten, 0), (spread, 1), (relay, 2), (share, 3), (send, 3)]
+    stages = [(whiten, 0), (relay, 2), (spread, 1), (share, 3), (send, 3)]
     if pass_on:
         stages.append((hand_on, 5))
 
@@ -349,13 +361,14 @@
 
 
 def variant_number(plan):
-    first, second = hop_of(plan[0]), hop_of(plan[1])
+    other = jnp.flip(plan)
+    first, second = hop_of(plan), hop_of(other)
     low, high = jnp.minimum(first, second), jnp.maximum(first, second)
-    change = plan[0] ^ plan[1]
+    change = plan ^ other
     direct = (high * (high + 1) >> 1) + low
     turned_off = 13 + ((high & 1) << 1) + (change & 1)
     relayed = jnp.where(low == high, 9 + high, turned_off)
-    return jnp.where((change < X_LO) & (low != 0) & (low * high != 3), relayed, direct)
+    return jnp.where((change < X_LO) & (low != 0) & (low * high != 3), relayed, direct)[0]
 
 
 def body(records, plan):

time: 147 us -> 135 us (0.918)
  Pallas kernels: 141 us -> 132 us
  between operations: 3.26 us -> 0.9 us
    pallas_call x1, Pallas kernels: 131 us -> 123 us  [exchange(): pl.pallas_call(functools.partial(exchange_kernel, *variant), out_shape=[j...]
where the time goes in v5:
time: 135 us
  Pallas kernels  132 us (98%)
    pallas_call x1, Pallas kernels, exchange(): pl.pallas_call(functools.partial(exchange_kernel, *variant), out_shape=[j...  123 us
    pallas_call x1, Pallas kernels, spectra(): pl.pallas_call(spectra_kernel, in_specs=[pl.BlockSpec(memory_space=pltpu....  9.37 us

profile of v5, /device:TPU:1, one launch (start us, length us, event | category | flops | bytes accessed | tf_op | source)
XLA Modules:
  0.0 135.3 jit_solution(5460864339677560230)
XLA Ops:
  0.6 0.7 rev.4
  1.4 0.7 and_select_fusion
  2.1 123.6 %conditional.1 = (bf16[8,512,512]{2,1,0:T(8,128)(2,1)S(1)}, bf16[2,8,512,512]{3,2,1,0:T(8,128)(2,1)S(1)}, bf16[8,10,128,256]{3,2,1,0:T(8,128)(2,1)S(1)}) conditional(s32[]{:T(128)} %bitcast.51, (bf16[64,64,512]{2,1,0:T(8,128)(2,1)}, s32[2]{0:T(128)}) %tuple.75, (bf16[64,64,512]{2,1,0:T(8,128)(2,1)}, ...), branch_computations={%region_0.1_spmd, %region_1.2_spmd, %region_2.3_spmd, %region_3.4_... | conditional | bytes 24 | solution.py:379
  2.3 122.8 %exchange_7.1 = (bf16[8,8,2,32,512]{4,3,2,1,0:T(8,128)(2,1)S(1)}, bf16[2,8,8,2,32,512]{5,4,3,2,1,0:T(8,128)(2,1)S(1)}, bf16[8,10,128,256]{3,2,1,0:T(8,128)(2,1)S(1)}) custom-call(s32[2]{0:T(128)} %get-tuple-element.103.plan_ref, bf16[8,16,32,512]{3,2,1,0:T(8,128)(2,1)} %bitcast.60), custom_call_target="tpu_custom_call" | custom-call | tf_op jit(solution)/shard_map/cond/branch_7_fun/exchange_7/pallas_call | solution.py:324
  125.7 9.4 %spectra.1 = (bf16[1,8,10,128,256]{4,3,2,1,0:T(8,128)(2,1)}, bf16[1,2,8,8,128,256]{5,4,3,2,1,0:T(8,128)(2,1)}) custom-call(s32[2]{0:T(128)} %plan_ref.1, bf16[8,512,512]{2,1,0:T(8,128)(2,1)S(1)} %get-tuple-element.158.own_ref, bf16[2,8,512,512]{3,2,1,0:T(8,128)(2,1)S(1)} %get-tuple-element.159.got_ref, ...), custom_call_target="tpu_custom_call" | custom-call | flops 5000000000 | bytes 14000000 | tf_op jit(solution)/shard_map/spectra/pallas_call | solution.py:92
